TPU v7x, 32 devices: a whole 2x2x4 slice. The times are simulated.
32 devices in a mesh: seq: 8 (over y, x, core), tp: 4 (over z).
Axes of the slice: x: 2, y: 2, z: 4, core: 2. Of those that a mesh axis runs over, the one named last changes fastest.
Arguments:
- hidden: bfloat16 [2048, 4096], P('seq', 'tp'), may hold values from -6 to 6
- norm_gain: float32 [4096], replicated, may hold values from 0.25 to 1.75
- value_weight: bfloat16 [4096, 4096], P(None, 'tp'), may hold values from -0.09375 to 0.09375
- gate_weight: bfloat16 [4096, 4096], P(None, 'tp'), may hold values from -0.09375 to 0.09375
- value_taps: float32 [3, 4096], P(None, 'tp'), may hold values from -3 to 3
- gate_taps: float32 [3, 4096], P(None, 'tp'), may hold values from -3 to 3
- rates: float32 [16, 4096], P(None, 'tp'), may hold values from 2.4414063e-05 to 0.05, as said below
- residues: float32 [16, 4096], P(None, 'tp'), may hold values from -1.5 to 1.5
- out_weight: bfloat16 [4096, 4096], P('tp'), may hold values from -0.125 to 0.125
Outputs:
- mixed: bfloat16 [2048, 4096], P('seq', 'tp')
Inputs may be any that keep to these rules, and one draw needn't show every extreme that they name: Decay rates are positive.
All inputs are finite; a program needn't handle non-finite values.
Results may differ from a plain program's by a relative error of at most 0.0076.
Values may be sent and summed in bfloat16 or wider, within the bound.
A program may use at most 256 MiB of HBM per device.

v0:
```python
import functools
import jax
import jax.numpy as jnp
from jax import lax
from jax.experimental import pallas as pl
from jax.experimental.pallas import tpu as pltpu
from jax.sharding import PartitionSpec as P

eps = 1e-05
f32 = jnp.float32
bf16 = jnp.bfloat16
LANES = 128
CHUNK = 16
HALF = CHUNK // 2
EDGE = 8
LIMIT = 56 * 1024 * 1024


def anti_identity(size):
    rows = lax.broadcasted_iota(jnp.int32, (size, size), 0)
    cols = lax.broadcasted_iota(jnp.int32, (size, size), 1)
    return (rows + cols == size - 1).astype(bf16)


def mirror(block, flip):
    size = flip.shape[0]
    count = block.shape[1] // size
    parts = [
        jnp.dot(block[:, (count - 1 - i) * size : (count - i) * size], flip, preferred_element_type=f32)
        for i in range(count)
    ]
    return jnp.concatenate(parts, axis=1) if count > 1 else parts[0]


def project_kernel(width, x_ref, far_ref, gain_ref, wv_ref, wg_ref, out_ref, both, acc, squares):
    step = pl.program_id(0)
    rows, depth = x_ref.shape[1], x_ref.shape[2]
    chans = wv_ref.shape[1]
    flip = anti_identity(min(256, depth))
    gain = gain_ref[...]
    values = x_ref[0].astype(f32)
    both[:rows] = (values * gain).astype(bf16)
    both[rows:] = (mirror(far_ref[0], flip) * gain).astype(bf16)
    part = jnp.sum(values * values, axis=1, keepdims=True)
    first = jnp.dot(both[...], wv_ref[...], preferred_element_type=f32)
    second = jnp.dot(both[...], wg_ref[...], preferred_element_type=f32)

    @pl.when(step == 0)
    def _():
        squares[...] = part
        acc[:, :chans] = first
        acc[:, chans:] = second

    @pl.when(step > 0)
    def _():
        squares[...] += part
        acc[:, :chans] += first
        acc[:, chans:] += second

    @pl.when(step == pl.num_programs(0) - 1)
    def _():
        scale = lax.rsqrt(squares[...] / width + eps)
        out_ref[0] = (acc[:rows] * scale).astype(bf16)
        out_ref[1] = (acc[rows:] * scale).astype(bf16)


def project(whole, gain, value_weight, gate_weight):
    owners, rows, chans = whole.shape
    width = owners * chans
    depth = min(512, chans)
    per = chans // depth
    steps = owners * per
    return pl.pallas_call(
        functools.partial(project_kernel, width),
        grid=(steps,),
        in_specs=[
            pl.BlockSpec((1, rows, depth), lambda i: (i // per, 0, i % per)),
            pl.BlockSpec((1, rows, depth), lambda i: ((steps - 1 - i) // per, 0, (steps - 1 - i) % per)),
            pl.BlockSpec((1, depth), lambda i: (0, i)),
            pl.BlockSpec((depth, chans), lambda i: (i, 0)),
            pl.BlockSpec((depth, chans), lambda i: (i, 0)),
        ],
        out_specs=pl.BlockSpec((2, rows, 2 * chans), lambda i: (0, 0, 0)),
        out_shape=jax.ShapeDtypeStruct((2, rows, 2 * chans), bf16),
        scratch_shapes=[
            pltpu.VMEM((2 * rows, depth), bf16),
            pltpu.VMEM((2 * rows, 2 * chans), f32),
            pltpu.VMEM((rows, 1), f32),
        ],
        compiler_params=pltpu.CompilerParams(vmem_limit_bytes=LIMIT),
        cost_estimate=pl.CostEstimate(
            flops=8 * rows * width * chans, bytes_accessed=4 * width * chans, transcendentals=0
        ),
        name="project",
    )(whole, whole, gain.reshape(1, width), value_weight, gate_weight)


def fill_tables(rates, cosh_ref, sinh_ref):
    for d in range(HALF):
        up = jnp.exp(rates * (d + 0.5))
        down = jnp.exp(rates * -(d + 0.5))
        cosh_ref[d] = 0.5 * (up + down)
        sinh_ref[d] = 0.5 * (up - down)


def smooth(wide, rows, taps, reverse):
    count = rows // CHUNK
    held = [wide[pl.ds(EDGE + s, count, stride=CHUNK), :] for s in range(-1, CHUNK + 1)]
    lead, mid, last = taps[0:1], taps[1:2], taps[2:3]
    if reverse:
        lead, last = last, lead
    return [lead * held[s] + mid * held[s + 1] + last * held[s + 2] for s in range(CHUNK)]


def pairs(signal):
    total = [signal[HALF + d] + signal[HALF - 1 - d] for d in range(HALF)]
    gap = [signal[HALF + d] - signal[HALF - 1 - d] for d in range(HALF)]
    return total, gap


def states_kernel(
    v_ref, g_ref, taps_ref, rates_ref, sent_ref, fore_ref, back_ref, wide, evens, odds, cosh_ref, sinh_ref
):
    rows = v_ref.shape[1]
    modes = rates_ref.shape[0]
    count = rows // CHUNK
    rates = rates_ref[...]
    taps = taps_ref[...]
    fill_tables(rates, cosh_ref, sinh_ref)
    centre = jnp.exp(rates * -(HALF - 0.5))
    leap = jnp.exp(rates * -float(CHUNK))
    totals = [[], []]
    zero = jnp.zeros((EDGE, LANES), f32)
    for strand in range(2):
        wide[:EDGE] = zero
        wide[EDGE + rows :] = zero
        wide[EDGE : EDGE + rows] = v_ref[strand].astype(f32)
        total, gap = pairs(smooth(wide, rows, taps, strand == 1))
        for m in range(modes):
            even = cosh_ref[0, m : m + 1] * total[0]
            odd = sinh_ref[0, m : m + 1] * gap[0]
            for d in range(1, HALF):
                even = even + cosh_ref[d, m : m + 1] * total[d]
                odd = odd + sinh_ref[d, m : m + 1] * gap[d]
            evens[m * count : (m + 1) * count] = even
            odds[m * count : (m + 1) * count] = odd
        state = jnp.zeros_like(rates)
        for n in range(count):
            fore_ref[strand, n] = state
            at = pl.ds(n, modes, stride=count)
            state = leap * state + centre * (evens[at, :] + odds[at, :])
        totals[0].append(state)
        state = jnp.zeros_like(rates)
        for n in reversed(range(count)):
            back_ref[strand, n] = state
            at = pl.ds(n, modes, stride=count)
            state = leap * state + centre * (evens[at, :] - odds[at, :])
        totals[1].append(state)
    edges = []
    for row in (0, rows - 1):
        for strand in range(2):
            for ref in (v_ref, g_ref):
                edges.append(ref[strand].astype(f32)[row : row + 1])
    edges.append(jnp.zeros((sent_ref.shape[0] - 4 * modes - 8, LANES), f32))
    sent_ref[...] = jnp.concatenate(totals[0] + totals[1] + edges, axis=0).astype(bf16)


def sent_rows(modes):
    return -(-(4 * modes + 8) // 16) * 16


def local_states(proj, value_taps, rates):
    _, rows, twice = proj.shape
    chans = twice // 2
    modes = rates.shape[0]
    count = rows // CHUNK
    tiles = chans // LANES
    sent = sent_rows(modes)
    states = jax.ShapeDtypeStruct((2, count, modes, chans), f32)
    state_spec = pl.BlockSpec((2, count, modes, LANES), lambda i: (0, 0, 0, i))
    return pl.pallas_call(
        states_kernel,
        grid=(tiles,),
        in_specs=[
            pl.BlockSpec((2, rows, LANES), lambda i: (0, 0, i)),
            pl.BlockSpec((2, rows, LANES), lambda i: (0, 0, i + tiles)),
            pl.BlockSpec((3, LANES), lambda i: (0, i)),
            pl.BlockSpec((modes, LANES), lambda i: (0, i)),
        ],
        out_specs=[pl.BlockSpec((sent, LANES), lambda i: (0, i)), state_spec, state_spec],
        out_shape=[jax.ShapeDtypeStruct((sent, chans), bf16), states, states],
        scratch_shapes=[
            pltpu.VMEM((rows + 2 * EDGE, LANES), f32),
            pltpu.VMEM((modes * count, LANES), f32),
            pltpu.VMEM((modes * count, LANES), f32),
            pltpu.VMEM((HALF, modes, LANES), f32),
            pltpu.VMEM((HALF, modes, LANES), f32),
        ],
        compiler_params=pltpu.CompilerParams(vmem_limit_bytes=LIMIT),
        name="local_states",
    )(proj, proj, value_taps, rates)


def gated_kernel(
    place_ref, v_ref, g_ref, vtaps_ref, gtaps_ref, rates_ref, res_ref, fore_ref, back_ref, all_ref,
    out_ref, wide, gate_wide, plus, minus, cosh_ref, sinh_ref, table, result,
):
    me = place_ref[0]
    devices = all_ref.shape[0]
    rows = v_ref.shape[1]
    modes = rates_ref.shape[0]
    count = rows // CHUNK
    rates = rates_ref[...]
    vtaps = vtaps_ref[...]
    gtaps = gtaps_ref[...]
    fill_tables(rates, cosh_ref, sinh_ref)
    strength = res_ref[...] * jnp.sqrt(rates)
    spread = strength * jnp.exp(rates * -(HALF + 0.5))
    behind = jnp.exp(rates)
    leap = jnp.exp(rates * -float(rows))
    across = jnp.exp(rates * -float(rows - 1))
    near = [
        0.5 * jnp.sum(strength * jnp.exp(rates * -float(k)), axis=0, keepdims=True)
        for k in range(CHUNK)
    ]
    for d in range(HALF):
        for e in range(HALF):
            at = d * HALF + e
            one, two = near[abs(d - e)], near[d + e + 1]
            table[at : at + 1] = one + two
            table[HALF * HALF + at : HALF * HALF + at + 1] = one - two

    def edge(source, which, strand, kind):
        at = 4 * modes + which * 4 + strand * 2 + kind
        return source[at : at + 1]

    gathered = [all_ref[src].astype(f32) for src in range(devices)]
    before = all_ref[jnp.maximum(me - 1, 0)].astype(f32) * (me > 0).astype(f32)
    after = all_ref[jnp.minimum(me + 1, devices - 1)].astype(f32) * (me < devices - 1).astype(f32)

    for strand in range(2):
        lead, last = (vtaps[0:1], vtaps[2:3]) if strand == 0 else (vtaps[2:3], vtaps[0:1])
        firsts = [
            lead * edge(gathered[src - 1], 1, strand, 0) if src else jnp.zeros((1, LANES), f32)
            for src in range(devices)
        ]
        lasts = [
            last * edge(gathered[src + 1], 0, strand, 0)
            if src < devices - 1
            else jnp.zeros((1, LANES), f32)
            for src in range(devices)
        ]
        fore = jnp.zeros_like(rates)
        for src in range(devices - 1):
            own = gathered[src][strand * modes : (strand + 1) * modes]
            own = own + across * firsts[src] + lasts[src]
            fore = jnp.where(src < me, fore * leap + own, fore)
        back = jnp.zeros_like(rates)
        for src in range(devices - 1, 0, -1):
            own = gathered[src][(2 + strand) * modes : (3 + strand) * modes]
            own = own + firsts[src] + across * lasts[src]
            back = jnp.where(src > me, back * leap + own, back)
        fore_on = fore + behind * (lead * edge(before, 1, strand, 0))
        back_on = back + behind * (last * edge(after, 0, strand, 0))
        for n in range(count):
            into = fore_ref[strand, n]
            into = into + (fore if n == 0 else jnp.exp(rates * -float(CHUNK * n)) * fore_on)
            outof = back_ref[strand, n]
            gap = count - 1 - n
            outof = outof + (back if gap == 0 else jnp.exp(rates * -float(CHUNK * gap)) * back_on)
            plus[n * modes : (n + 1) * modes] = spread * (into + outof)
            minus[n * modes : (n + 1) * modes] = spread * (into - outof)

        for buf, ref, kind in ((wide, v_ref, 0), (gate_wide, g_ref, 1)):
            buf[EDGE : EDGE + rows] = ref[strand].astype(f32)
            buf[EDGE - 1 : EDGE] = edge(before, 1, strand, kind)
            buf[EDGE + rows : EDGE + rows + 1] = edge(after, 0, strand, kind)
        total, gap = pairs(smooth(wide, rows, vtaps, strand == 1))
        even, odd = [], []
        for d in range(HALF):
            base = d * HALF
            one = table[base : base + 1] * total[0]
            two = table[HALF * HALF + base : HALF * HALF + base + 1] * gap[0]
            for e in range(1, HALF):
                at = base + e
                one = one + table[at : at + 1] * total[e]
                two = two + table[HALF * HALF + at : HALF * HALF + at + 1] * gap[e]
            even.append(one)
            odd.append(two)
        for m in range(modes):
            add = plus[pl.ds(m, count, stride=modes), :]
            sub = minus[pl.ds(m, count, stride=modes), :]
            for d in range(HALF):
                even[d] = even[d] + cosh_ref[d, m : m + 1] * add
                odd[d] = odd[d] - sinh_ref[d, m : m + 1] * sub
        gates = smooth(gate_wide, rows, gtaps, strand == 1)
        for d in range(HALF):
            one, two = HALF + d, HALF - 1 - d
            result[pl.ds(one, count, stride=CHUNK), :] = gates[one] * (even[d] + odd[d])
            result[pl.ds(two, count, stride=CHUNK), :] = gates[two] * (even[d] - odd[d])
        out_ref[strand] = result[...].astype(bf16)


def gated(place, proj, value_taps, gate_taps, rates, residues, fore, back, everyone):
    _, rows, twice = proj.shape
    chans = twice // 2
    modes = rates.shape[0]
    count = rows // CHUNK
    tiles = chans // LANES
    devices, sent, _ = everyone.shape
    state_spec = pl.BlockSpec((2, count, modes, LANES), lambda i: (0, 0, 0, i))
    tap_spec = pl.BlockSpec((3, LANES), lambda i: (0, i))
    mode_spec = pl.BlockSpec((modes, LANES), lambda i: (0, i))
    return pl.pallas_call(
        gated_kernel,
        grid=(tiles,),
        in_specs=[
            pl.BlockSpec(memory_space=pltpu.SMEM),
            pl.BlockSpec((2, rows, LANES), lambda i: (0, 0, i)),
            pl.BlockSpec((2, rows, LANES), lambda i: (0, 0, i + tiles)),
            tap_spec,
            tap_spec,
            mode_spec,
            mode_spec,
            state_spec,
            state_spec,
            pl.BlockSpec((devices, sent, LANES), lambda i: (0, 0, i)),
        ],
        out_specs=pl.BlockSpec((2, rows, LANES), lambda i: (0, 0, i)),
        out_shape=jax.ShapeDtypeStruct((2, rows, chans), bf16),
        scratch_shapes=[
            pltpu.VMEM((rows + 2 * EDGE, LANES), f32),
            pltpu.VMEM((rows + 2 * EDGE, LANES), f32),
            pltpu.VMEM((modes * count, LANES), f32),
            pltpu.VMEM((modes * count, LANES), f32),
            pltpu.VMEM((HALF, modes, LANES), f32),
            pltpu.VMEM((HALF, modes, LANES), f32),
            pltpu.VMEM((2 * HALF * HALF, LANES), f32),
            pltpu.VMEM((rows, LANES), f32),
        ],
        compiler_params=pltpu.CompilerParams(vmem_limit_bytes=LIMIT),
        name="gated",
    )(place, proj, proj, value_taps, gate_taps, rates, residues, fore, back, everyone)


def output_kernel(z_ref, low_ref, high_ref, out_ref):
    step = pl.program_id(0)
    _, rows, chans = z_ref.shape
    size = low_ref.shape[1]
    per = out_ref.shape[2] // size
    tiles = 2 * pl.num_programs(0)
    flip = anti_identity(min(256, size))

    def turned(product):
        high = product.astype(bf16)
        low = (product - high.astype(f32)).astype(bf16)
        return mirror(high, flip) + mirror(low, flip)

    z = z_ref[...].reshape(2 * rows, chans)
    low = jnp.dot(z, low_ref[...], preferred_element_type=f32)
    high = jnp.dot(z, high_ref[...], preferred_element_type=f32)
    other = tiles - 1 - step
    for tile, own, far in ((step, low, high), (other, high, low)):
        cols = pl.ds(pl.multiple_of(lax.rem(tile, per) * size, size), size)
        out_ref[tile // per, :, cols] = (own[:rows] + turned(far[rows:])).astype(bf16)


def output(z, out_weight, parts):
    _, rows, chans = z.shape
    width = out_weight.shape[1]
    each = width // parts
    size = min(512, each)
    tiles = width // size
    return pl.pallas_call(
        output_kernel,
        grid=(tiles // 2,),
        in_specs=[
            pl.BlockSpec((2, rows, chans), lambda i: (0, 0, 0)),
            pl.BlockSpec((chans, size), lambda i: (0, i)),
            pl.BlockSpec((chans, size), lambda i: (0, tiles - 1 - i)),
        ],
        out_specs=pl.BlockSpec((parts, rows, each), lambda i: (0, 0, 0)),
        out_shape=jax.ShapeDtypeStruct((parts, rows, each), bf16),
        compiler_params=pltpu.CompilerParams(vmem_limit_bytes=LIMIT),
        name="output",
    )(z, out_weight, out_weight)


def body(
    hidden, norm_gain, value_weight, gate_weight, value_taps, gate_taps, rates, residues, out_weight
):
    whole = lax.all_gather(hidden, "tp", axis=0)
    proj = project(whole, norm_gain, value_weight, gate_weight)
    sent, fore, back = local_states(proj, value_taps, rates)
    everyone = lax.all_gather(sent, "seq", axis=0)
    place = lax.axis_index("seq").astype(jnp.int32).reshape(1)
    z = gated(place, proj, value_taps, gate_taps, rates, residues, fore, back, everyone)
    term = output(z, out_weight, lax.axis_size("tp"))
    return lax.psum_scatter(term, "tp", scatter_dimension=0, tiled=False)


def solution(mesh):
    in_specs = (
        P("seq", "tp"),
        P(),
        P(None, "tp"),
        P(None, "tp"),
        P(None, "tp"),
        P(None, "tp"),
        P(None, "tp"),
        P(None, "tp"),
        P("tp", None),
    )
    out_specs = P("seq", "tp")
    return jax.shard_map(body, mesh=mesh, in_specs=in_specs, out_specs=out_specs, check_vma=False)
```

profile of v0, /device:TPU:0, one launch (start us, length us, event | category | flops | bytes accessed | tf_op | source)
XLA Modules:
  0.0 179.0 jit_solution(5482518305388209803)
XLA Ops:
  6.5 0.0 all-gather.5.cloned.1.call-start
  6.5 0.7 all-gather.5.cloned.1.call-update
  7.3 0.0 all-gather.7.cloned.1.call-start
  7.3 50.3 %all-gather.5.cloned.1.call-done = bf16[1024,1024]{1,0:T(8,128)(2,1)} async-done(((bf16[256,1024]{1,0:T(8,128)(2,1)}), bf16[1024,1024]{1,0:T(8,128)(2,1)}) %all-gather.5.cloned.1.call-update) | async-done | bytes 2097168 | tf_op jit(solution)/shard_map/all_gather | solution.py:392
  57.6 17.7 %project.1.v_ref.g_ref = bf16[2,256,2048]{2,1,0:T(8,128)(2,1)} custom-call(bf16[4,256,1024]{2,1,0:T(8,128)(2,1)} %bitcast.6, bf16[4,256,1024]{2,1,0:T(8,128)(2,1)} %bitcast.7, f32[1,4096]{1,0:T(1,128)} %bitcast.8, bf16[4096,1024]{1,0:T(8,128)(2,1)} %wv_ref.1, bf16[4096,1024]{1,0:T(8,128)(2,1)} %wg_ref.1), custom_call_target="tpu_custom_call" | custom-call | flops 8589934592 | bytes 16777216 | tf_op jit(solution)/shard_map/project/pallas_call | solution.py:73
  75.3 8.4 %local_states.1 = (bf16[80,1024]{1,0:T(8,128)(2,1)}, f32[2,16,16,1024]{3,2,1,0:T(8,128)}, f32[2,16,16,1024]{3,2,1,0:T(8,128)}) custom-call(bf16[2,256,2048]{2,1,0:T(8,128)(2,1)} %project.1.v_ref.g_ref, bf16[2,256,2048]{2,1,0:T(8,128)(2,1)} %project.1.v_ref.g_ref, f32[3,1024]{1,0:T(4,128)} %vtaps_ref.1, f32[16,1024]{1,0:T(8,128)} %rates_ref.3), custom_call_target="tpu_custom_call" | custom-call | tf_op jit(solution)/shard_map/local_states/pallas_call | solution.py:181
  83.8 0.0 all-gather.7.cloned.1.call-update
  83.8 0.0 reduce-scatter.2.cloned.1.call-start
  83.9 23.4 %all-gather.7.cloned.1.call-done = bf16[640,1024]{1,0:T(8,128)(2,1)} async-done(((bf16[80,1024]{1,0:T(8,128)(2,1)}), bf16[640,1024]{1,0:T(8,128)(2,1)}) %all-gather.7.cloned.1.call-update) | async-done | bytes 1310736 | tf_op jit(solution)/shard_map/all_gather | solution.py:395
  107.3 11.5 %gated.1.z_ref = bf16[2,256,1024]{2,1,0:T(8,128)(2,1)} custom-call(s32[1]{0:T(128)} %bitcast.place_ref, bf16[2,256,2048]{2,1,0:T(8,128)(2,1)} %project.1.v_ref.g_ref, bf16[2,256,2048]{2,1,0:T(8,128)(2,1)} %project.1.v_ref.g_ref, f32[3,1024]{1,0:T(4,128)} %vtaps_ref.1, f32[3,1024]{1,0:T(4,128)} %gtaps_ref.1, f32[16,1024]{1,0:T(8,128)} %rates_ref.3, ...), custom_call_target="tpu_custom_call" | custom-call | tf_op jit(solution)/shard_map/gated/pallas_call | solution.py:314
  118.7 9.7 %output.1 = bf16[4,256,1024]{2,1,0:T(8,128)(2,1)} custom-call(bf16[2,256,1024]{2,1,0:T(8,128)(2,1)} %gated.1.z_ref, bf16[1024,4096]{1,0:T(8,128)(2,1)} %high_ref.1, bf16[1024,4096]{1,0:T(8,128)(2,1)} %high_ref.1), custom_call_target="tpu_custom_call" | custom-call | tf_op jit(solution)/shard_map/output/pallas_call | solution.py:374
  128.4 0.0 reduce-scatter.2.cloned.1.call-update
  128.5 44.0 %reduce-scatter.2.cloned.1.call-done = bf16[1,256,1024]{2,1,0:T(8,128)(2,1)} async-done(((bf16[4,256,1024]{2,1,0:T(8,128)(2,1)}), bf16[1,256,1024]{2,1,0:T(8,128)(2,1)}) %reduce-scatter.2.cloned.1.call-update) | async-done | bytes 524304 | tf_op jit(solution)/shard_map/reduce_scatter | solution.py:399
Async XLA Ops:
  6.5 51.1 %all-gather.5.cloned.1.call-start = ((), (), s32[]{:S(2)}) async-start(), calls=%async_computation.2 | async-start | bytes 2621440 | tf_op jit(solution)/shard_map/all_gather | solution.py:392
  7.3 100.0 %all-gather.7.cloned.1.call-start = ((), (), s32[]{:S(2)}) async-start(), calls=%async_computation.3 | async-start | bytes 1474560 | tf_op jit(solution)/shard_map/all_gather | solution.py:395
  83.8 88.7 %reduce-scatter.2.cloned.1.call-start = ((), (), s32[]{:S(2)}) async-start(), calls=%async_computation.1 | async-start | bytes 2621440 | tf_op jit(solution)/shard_map/reduce_scatter | solution.py:399
Sparse Core Ops, SparseCore 0:
  8.9 48.6 all-gather.4
  83.9 23.2 all-gather.6
  128.6 43.8 reduce-scatter.1
where the time goes:
time: 179 us
  waiting for transfers between devices  118 us (66%)
  Pallas kernels  47.3 us (26%)
  between operations  13.1 us (7%)
    all_gather x1, waiting for transfers between devices, body(): whole = lax.all_gather(hidden, 'tp', axis=0)  50.3 us
    reduce_scatter x1, waiting for transfers between devices, body(): return lax.psum_scatter(term, 'tp', scatter_dimension=0, tiled=False)  44 us
    all_gather x1, waiting for transfers between devices, body(): everyone = lax.all_gather(sent, 'seq', axis=0)  23.4 us
    pallas_call x1, Pallas kernels, project(): pl.pallas_call(functools.partial(project_kernel, width), grid=(steps,), i...  17.7 us
    pallas_call x1, Pallas kernels, gated(): pl.pallas_call(gated_kernel, grid=(tiles,), in_specs=[pl.BlockSpec(memory...  11.5 us
    pallas_call x1, Pallas kernels, output(): pl.pallas_call(output_kernel, grid=(tiles // 2,), in_specs=[pl.BlockSpec(...  9.7 us
    pallas_call x1, Pallas kernels, local_states(): pl.pallas_call(states_kernel, grid=(tiles,), in_specs=[pl.BlockSpec((2, r...  8.45 us
  transfers between devices with their start and end apart: 3, of which 3 were waited for; matrix products, arithmetic and copies ran while one was open for 0% of the time, Pallas kernels for 0%

commit v1 on v0

--- a/solution.py
+++ b/solution.py
@@ -32,67 +32,58 @@
     return jnp.concatenate(parts, axis=1) if count > 1 else parts[0]
 
 
-def project_kernel(width, x_ref, far_ref, gain_ref, wv_ref, wg_ref, out_ref, both, acc, squares):
-    step = pl.program_id(0)
-    rows, depth = x_ref.shape[1], x_ref.shape[2]
-    chans = wv_ref.shape[1]
-    flip = anti_identity(min(256, depth))
-    gain = gain_ref[...]
-    values = x_ref[0].astype(f32)
-    both[:rows] = (values * gain).astype(bf16)
-    both[rows:] = (mirror(far_ref[0], flip) * gain).astype(bf16)
-    part = jnp.sum(values * values, axis=1, keepdims=True)
-    first = jnp.dot(both[...], wv_ref[...], preferred_element_type=f32)
-    second = jnp.dot(both[...], wg_ref[...], preferred_element_type=f32)
-
-    @pl.when(step == 0)
+def project_kernel(x_ref, gain_ref, wv_ref, wg_ref, *rest):
+    v_ref, g_ref, both = rest[-3:]
+    owners, rows, chans = x_ref.shape
+
+    @pl.when(pl.program_id(0) == 0)
     def _():
-        squares[...] = part
-        acc[:, :chans] = first
-        acc[:, chans:] = second
-
-    @pl.when(step > 0)
-    def _():
-        squares[...] += part
-        acc[:, :chans] += first
-        acc[:, chans:] += second
-
-    @pl.when(step == pl.num_programs(0) - 1)
-    def _():
-        scale = lax.rsqrt(squares[...] / width + eps)
-        out_ref[0] = (acc[:rows] * scale).astype(bf16)
-        out_ref[1] = (acc[rows:] * scale).astype(bf16)
-
-
-def project(whole, gain, value_weight, gate_weight):
+        flip = anti_identity(min(256, chans))
+        squares = jnp.zeros((rows, 1), f32)
+        for owner in range(owners):
+            values = x_ref[owner].astype(f32)
+            squares = squares + jnp.sum(values * values, axis=1, keepdims=True)
+        scale = lax.rsqrt(squares / (owners * chans) + eps)
+        for owner in range(owners):
+            cols = slice(owner * chans, (owner + 1) * chans)
+            gain = gain_ref[:, cols]
+            both[:rows, cols] = (x_ref[owner].astype(f32) * scale * gain).astype(bf16)
+            far = mirror(x_ref[owners - 1 - owner], flip)
+            both[rows:, cols] = (far * scale * gain).astype(bf16)
+
+    for weight_ref, out_ref in ((wv_ref, v_ref), (wg_ref, g_ref)):
+        product = jnp.dot(both[...], weight_ref[...], preferred_element_type=f32).astype(bf16)
+        out_ref[0] = product[:rows]
+        out_ref[1] = product[rows:]
+
+
+def project(whole, part, parts, gain, value_weight, gate_weight, earlier):
     owners, rows, chans = whole.shape
     width = owners * chans
-    depth = min(512, chans)
-    per = chans // depth
-    steps = owners * per
+    size = min(256, chans)
+    weight_spec = pl.BlockSpec((width, size), lambda i: (0, i))
+    out_spec = pl.BlockSpec((2, rows, size), lambda i: (0, part, i))
+    out_shape = jax.ShapeDtypeStruct((2, rows * parts, chans), bf16)
     return pl.pallas_call(
-        functools.partial(project_kernel, width),
-        grid=(steps,),
+        project_kernel,
+        grid=(chans // size,),
         in_specs=[
-            pl.BlockSpec((1, rows, depth), lambda i: (i // per, 0, i % per)),
-            pl.BlockSpec((1, rows, depth), lambda i: ((steps - 1 - i) // per, 0, (steps - 1 - i) % per)),
-            pl.BlockSpec((1, depth), lambda i: (0, i)),
-            pl.BlockSpec((depth, chans), lambda i: (i, 0)),
-            pl.BlockSpec((depth, chans), lambda i: (i, 0)),
-        ],
-        out_specs=pl.BlockSpec((2, rows, 2 * chans), lambda i: (0, 0, 0)),
-        out_shape=jax.ShapeDtypeStruct((2, rows, 2 * chans), bf16),
-        scratch_shapes=[
-            pltpu.VMEM((2 * rows, depth), bf16),
-            pltpu.VMEM((2 * rows, 2 * chans), f32),
-            pltpu.VMEM((rows, 1), f32),
-        ],
+            pl.BlockSpec((owners, rows, chans), lambda i: (0, 0, 0)),
+            pl.BlockSpec((1, width), lambda i: (0, 0)),
+            weight_spec,
+            weight_spec,
+        ]
+        + [pl.BlockSpec(memory_space=pl.ANY)] * len(earlier),
+        out_specs=[out_spec, out_spec],
+        out_shape=[out_shape, out_shape],
+        input_output_aliases={4 + i: i for i in range(len(earlier))},
+        scratch_shapes=[pltpu.VMEM((2 * rows, width), bf16)],
         compiler_params=pltpu.CompilerParams(vmem_limit_bytes=LIMIT),
         cost_estimate=pl.CostEstimate(
             flops=8 * rows * width * chans, bytes_accessed=4 * width * chans, transcendentals=0
         ),
         name="project",
-    )(whole, whole, gain.reshape(1, width), value_weight, gate_weight)
+    )(whole, gain.reshape(1, width), value_weight, gate_weight, *earlier)
 
 
 def fill_tables(rates, cosh_ref, sinh_ref):
@@ -169,9 +160,8 @@
     return -(-(4 * modes + 8) // 16) * 16
 
 
-def local_states(proj, value_taps, rates):
-    _, rows, twice = proj.shape
-    chans = twice // 2
+def local_states(values, gates, value_taps, rates):
+    _, rows, chans = values.shape
     modes = rates.shape[0]
     count = rows // CHUNK
     tiles = chans // LANES
@@ -183,7 +173,7 @@
         grid=(tiles,),
         in_specs=[
             pl.BlockSpec((2, rows, LANES), lambda i: (0, 0, i)),
-            pl.BlockSpec((2, rows, LANES), lambda i: (0, 0, i + tiles)),
+            pl.BlockSpec((2, rows, LANES), lambda i: (0, 0, i)),
             pl.BlockSpec((3, LANES), lambda i: (0, i)),
             pl.BlockSpec((modes, LANES), lambda i: (0, i)),
         ],
@@ -198,7 +188,7 @@
         ],
         compiler_params=pltpu.CompilerParams(vmem_limit_bytes=LIMIT),
         name="local_states",
-    )(proj, proj, value_taps, rates)
+    )(values, gates, value_taps, rates)
 
 
 def gated_kernel(
@@ -301,9 +291,8 @@
         out_ref[strand] = result[...].astype(bf16)
 
 
-def gated(place, proj, value_taps, gate_taps, rates, residues, fore, back, everyone):
-    _, rows, twice = proj.shape
-    chans = twice // 2
+def gated(place, values, gates, value_taps, gate_taps, rates, residues, fore, back, everyone):
+    _, rows, chans = values.shape
     modes = rates.shape[0]
     count = rows // CHUNK
     tiles = chans // LANES
@@ -317,7 +306,7 @@
         in_specs=[
             pl.BlockSpec(memory_space=pltpu.SMEM),
             pl.BlockSpec((2, rows, LANES), lambda i: (0, 0, i)),
-            pl.BlockSpec((2, rows, LANES), lambda i: (0, 0, i + tiles)),
+            pl.BlockSpec((2, rows, LANES), lambda i: (0, 0, i)),
             tap_spec,
             tap_spec,
             mode_spec,
@@ -340,7 +329,7 @@
         ],
         compiler_params=pltpu.CompilerParams(vmem_limit_bytes=LIMIT),
         name="gated",
-    )(place, proj, proj, value_taps, gate_taps, rates, residues, fore, back, everyone)
+    )(place, values, gates, value_taps, gate_taps, rates, residues, fore, back, everyone)
 
 
 def output_kernel(z_ref, low_ref, high_ref, out_ref):
@@ -389,12 +378,18 @@
 def body(
     hidden, norm_gain, value_weight, gate_weight, value_taps, gate_taps, rates, residues, out_weight
 ):
-    whole = lax.all_gather(hidden, "tp", axis=0)
-    proj = project(whole, norm_gain, value_weight, gate_weight)
-    sent, fore, back = local_states(proj, value_taps, rates)
+    parts = 2
+    rows = hidden.shape[0] // parts
+    wholes = [
+        lax.all_gather(hidden[part * rows : (part + 1) * rows], "tp", axis=0) for part in range(parts)
+    ]
+    proj = ()
+    for part, whole in enumerate(wholes):
+        proj = project(whole, part, parts, norm_gain, value_weight, gate_weight, proj)
+    sent, fore, back = local_states(*proj, value_taps, rates)
     everyone = lax.all_gather(sent, "seq", axis=0)
     place = lax.axis_index("seq").astype(jnp.int32).reshape(1)
-    z = gated(place, proj, value_taps, gate_taps, rates, residues, fore, back, everyone)
+    z = gated(place, *proj, value_taps, gate_taps, rates, residues, fore, back, everyone)
     term = output(z, out_weight, lax.axis_size("tp"))
     return lax.psum_scatter(term, "tp", scatter_dimension=0, tiled=False)
 

time: 179 us -> 184 us (1.028)
  Pallas kernels: 47.3 us -> 50.7 us
  local copies, waits for them, and re-layouts: 0 us -> 1.84 us
    pallas_call x1 -> x2, Pallas kernels: 17.7 us -> 21.2 us  [project(): pl.pallas_call(project_kernel, grid=(chans // size,), in_specs=[pl.BlockS...]
    slice x0 -> x1, local copies, waits for them, and re-layouts: none -> 1.84 us  [body(): hidden[part * rows:(part + 1) * rows]]
    all_gather x1 -> x2, waiting for transfers between devices: 50.3 us -> 48.8 us  [body(): lax.all_gather(hidden[part * rows:(part + 1) * rows], 'tp', axis=0)]
  transfers between devices with their start and end apart: 3 -> 4, of which waited for: 3 -> 4; matrix products, arithmetic and copies ran while one was open for 0% -> 0% of each run, Pallas kernels for 0% -> 6%
where the time goes in v1:
time: 184 us
  waiting for transfers between devices  118 us (64%)
  Pallas kernels  50.7 us (28%)
  between operations  13.1 us (7%)
  local copies, waits for them, and re-layouts  1.84 us (1%)
    all_gather x2, waiting for transfers between devices, body(): lax.all_gather(hidden[part * rows:(part + 1) * rows], 'tp', axis=0)  48.8 us
    reduce_scatter x1, waiting for transfers between devices, body(): return lax.psum_scatter(term, 'tp', scatter_dimension=0, tiled=False)  44 us
    all_gather x1, waiting for transfers between devices, body(): everyone = lax.all_gather(sent, 'seq', axis=0)  24.2 us
    pallas_call x2, Pallas kernels, project(): pl.pallas_call(project_kernel, grid=(chans // size,), in_specs=[pl.BlockS...  21.2 us
    pallas_call x1, Pallas kernels, gated(): pl.pallas_call(gated_kernel, grid=(tiles,), in_specs=[pl.BlockSpec(memory...  11.4 us
    pallas_call x1, Pallas kernels, output(): pl.pallas_call(output_kernel, grid=(tiles // 2,), in_specs=[pl.BlockSpec(...  9.68 us
    pallas_call x1, Pallas kernels, local_states(): pl.pallas_call(states_kernel, grid=(tiles,), in_specs=[pl.BlockSpec((2, r...  8.42 us
  transfers between devices with their start and end apart: 4, of which 4 were waited for; matrix products, arithmetic and copies ran while one was open for 0% of the time, Pallas kernels for 6%

profile of v1, /device:TPU:0, one launch (start us, length us, event | category | flops | bytes accessed | tf_op | source)
XLA Modules:
  0.0 183.5 jit_solution(11670660014264234216)
XLA Ops:
  6.5 0.0 all-gather.9.cloned.1.call-start
  6.5 1.8 %fusion = (bf16[128,1024]{1,0:T(8,128)(2,1)}, bf16[128,1024]{1,0:T(8,128)(2,1)}) fusion(bf16[256,1024]{1,0:T(8,128)(2,1)} %param.9), kind=kLoop, calls=%fused_computation | loop fusion | bytes 1048576 | tf_op jit(solution)/shard_map/slice | solution.py:384
  8.4 0.0 all-gather.9.cloned.1.call-update
  8.4 0.0 all-gather.7.cloned.1.call-start
  8.5 0.7 all-gather.7.cloned.1.call-update
  9.2 0.0 all-gather.11.cloned.1.call-start
  9.2 30.4 %all-gather.9.cloned.1.call-done = bf16[512,1024]{1,0:T(8,128)(2,1)} async-done(((bf16[128,1024]{1,0:T(8,128)(2,1)}), bf16[512,1024]{1,0:T(8,128)(2,1)}) %all-gather.9.cloned.1.call-update) | async-done | bytes 1048592 | tf_op jit(solution)/shard_map/all_gather | solution.py:384
  39.6 10.6 %project.2 = (bf16[2,256,1024]{2,1,0:T(8,128)(2,1)}, bf16[2,256,1024]{2,1,0:T(8,128)(2,1)}) custom-call(bf16[4,128,1024]{2,1,0:T(8,128)(2,1)} %bitcast.7, f32[1,4096]{1,0:T(1,128)} %bitcast.9, bf16[4096,1024]{1,0:T(8,128)(2,1)} %wv_ref.3, bf16[4096,1024]{1,0:T(8,128)(2,1)} %wg_ref.3), custom_call_target="tpu_custom_call" | custom-call | flops 4294967296 | bytes 16777216 | tf_op jit(solution)/shard_map/project/pallas_call | solution.py:67
  50.2 18.4 %all-gather.7.cloned.1.call-done = bf16[512,1024]{1,0:T(8,128)(2,1)} async-done(((bf16[128,1024]{1,0:T(8,128)(2,1)}), bf16[512,1024]{1,0:T(8,128)(2,1)}) %all-gather.7.cloned.1.call-update) | async-done | bytes 1048592 | tf_op jit(solution)/shard_map/all_gather | solution.py:384
  68.6 10.5 %project.3 = (bf16[2,256,1024]{2,1,0:T(8,128)(2,1)}, bf16[2,256,1024]{2,1,0:T(8,128)(2,1)}) custom-call(bf16[4,128,1024]{2,1,0:T(8,128)(2,1)} %bitcast.8, f32[1,4096]{1,0:T(1,128)} %bitcast.10, bf16[4096,1024]{1,0:T(8,128)(2,1)} %wv_ref.3, bf16[4096,1024]{1,0:T(8,128)(2,1)} %wg_ref.3, ...), custom_call_target="tpu_custom_call", output_to_operand_aliasing={{0}: (4, {}), {1}: (5, {})} | custom-call | flops 4294967296 | bytes 16777216 | tf_op jit(solution)/shard_map/project/pallas_call | solution.py:67
  79.2 8.4 %local_states.1 = (bf16[80,1024]{1,0:T(8,128)(2,1)}, f32[2,16,16,1024]{3,2,1,0:T(8,128)}, f32[2,16,16,1024]{3,2,1,0:T(8,128)}) custom-call(bf16[2,256,1024]{2,1,0:T(8,128)(2,1)} %get-tuple-element.14.v_ref, bf16[2,256,1024]{2,1,0:T(8,128)(2,1)} %get-tuple-element.15.g_ref, f32[3,1024]{1,0:T(4,128)} %vtaps_ref.1, f32[16,1024]{1,0:T(8,128)} %rates_ref.3), custom_call_target="tpu_custom_call" | custom-call | tf_op jit(solution)/shard_map/local_states/pallas_call | solution.py:171
  87.6 0.0 all-gather.11.cloned.1.call-update
  87.6 0.0 reduce-scatter.2.cloned.1.call-start
  87.7 24.2 %all-gather.11.cloned.1.call-done = bf16[640,1024]{1,0:T(8,128)(2,1)} async-done(((bf16[80,1024]{1,0:T(8,128)(2,1)}), bf16[640,1024]{1,0:T(8,128)(2,1)}) %all-gather.11.cloned.1.call-update) | async-done | bytes 1310736 | tf_op jit(solution)/shard_map/all_gather | solution.py:390
  111.9 11.4 %gated.1.z_ref = bf16[2,256,1024]{2,1,0:T(8,128)(2,1)} custom-call(s32[1]{0:T(128)} %bitcast.place_ref, bf16[2,256,1024]{2,1,0:T(8,128)(2,1)} %get-tuple-element.14.v_ref, bf16[2,256,1024]{2,1,0:T(8,128)(2,1)} %get-tuple-element.15.g_ref, f32[3,1024]{1,0:T(4,128)} %vtaps_ref.1, f32[3,1024]{1,0:T(4,128)} %gtaps_ref.1, f32[16,1024]{1,0:T(8,128)} %rates_ref.3, ...), custom_call_target="tpu_custom_call" | custom-call | tf_op jit(solution)/shard_map/gated/pallas_call | solution.py:303
  123.3 9.7 %output.1 = bf16[4,256,1024]{2,1,0:T(8,128)(2,1)} custom-call(bf16[2,256,1024]{2,1,0:T(8,128)(2,1)} %gated.1.z_ref, bf16[1024,4096]{1,0:T(8,128)(2,1)} %high_ref.1, bf16[1024,4096]{1,0:T(8,128)(2,1)} %high_ref.1), custom_call_target="tpu_custom_call" | custom-call | tf_op jit(solution)/shard_map/output/pallas_call | solution.py:363
  133.0 0.0 reduce-scatter.2.cloned.1.call-update
  133.0 44.0 %reduce-scatter.2.cloned.1.call-done = bf16[1,256,1024]{2,1,0:T(8,128)(2,1)} async-done(((bf16[4,256,1024]{2,1,0:T(8,128)(2,1)}), bf16[1,256,1024]{2,1,0:T(8,128)(2,1)}) %reduce-scatter.2.cloned.1.call-update) | async-done | bytes 524304 | tf_op jit(solution)/shard_map/reduce_scatter | solution.py:394
Async XLA Ops:
  6.5 33.1 %all-gather.9.cloned.1.call-start = ((), (), s32[]{:S(2)}) async-start(), calls=%async_computation.3 | async-start | bytes 1310720 | tf_op jit(solution)/shard_map/all_gather | solution.py:384
  8.4 60.2 %all-gather.7.cloned.1.call-start = ((), (), s32[]{:S(2)}) async-start(), calls=%async_computation.2 | async-start | bytes 1310720 | tf_op jit(solution)/shard_map/all_gather | solution.py:384
  9.2 102.7 %all-gather.11.cloned.1.call-start = ((), (), s32[]{:S(2)}) async-start(), calls=%async_computation.4 | async-start | bytes 1474560 | tf_op jit(solution)/shard_map/all_gather | solution.py:390
  87.6 89.4 %reduce-scatter.2.cloned.1.call-start = ((), (), s32[]{:S(2)}) async-start(), calls=%async_computation.1 | async-start | bytes 2621440 | tf_op jit(solution)/shard_map/reduce_scatter | solution.py:394
Sparse Core Ops, SparseCore 0:
  8.9 30.6 all-gather.8
  41.2 27.4 all-gather.6
  87.7 24.0 all-gather.10
  133.1 43.8 reduce-scatter.1

commit v2 on v1

--- a/solution.py
+++ b/solution.py
@@ -30,6 +30,110 @@
         for i in range(count)
     ]
     return jnp.concatenate(parts, axis=1) if count > 1 else parts[0]
+
+
+MESH = pl.DeviceIdType.MESH
+
+
+def line_kernel(axis, count, x_ref, out_ref, to_right, to_left, landed, own_sem):
+    me = lax.axis_index(axis)
+    has_left, has_right = me > 0, me < count - 1
+    left, right = jnp.maximum(me - 1, 0), jnp.minimum(me + 1, count - 1)
+    barrier = pltpu.get_barrier_semaphore()
+    for hop in range(1, count):
+        other = lax.rem(me + hop, count)
+        pl.semaphore_signal(barrier, inc=1, device_id={axis: other}, device_id_type=MESH)
+    pl.semaphore_wait(barrier, count - 1)
+
+    def move(step, block, rightward):
+        sems, target = (to_right, right) if rightward else (to_left, left)
+        return pltpu.make_async_remote_copy(
+            src_ref=x_ref if step == 0 else out_ref.at[block],
+            dst_ref=out_ref.at[block],
+            send_sem=sems.at[step],
+            recv_sem=landed.at[block],
+            device_id={axis: target},
+            device_id_type=MESH,
+        )
+
+    own = pltpu.make_async_copy(x_ref, out_ref.at[me], own_sem)
+    for step in range(count):
+        for rightward in (True, False):
+            block = me - step if rightward else me + step
+            exists = block >= 0 if rightward else block < count
+            onward = has_right if rightward else has_left
+
+            if step > 0:
+
+                @pl.when(exists)
+                def _():
+                    move(step, block, rightward).wait_recv()
+
+            if step < count - 1:
+
+                @pl.when(jnp.logical_and(exists, onward))
+                def _():
+                    move(step, block, rightward).start()
+
+        if step == 0:
+            own.start()
+    for step in range(count - 1):
+        for rightward in (True, False):
+            block = me - step if rightward else me + step
+            exists = block >= 0 if rightward else block < count
+            onward = has_right if rightward else has_left
+
+            @pl.when(jnp.logical_and(exists, onward))
+            def _():
+                move(step, block, rightward).wait_send()
+
+    own.wait()
+
+
+def direct_kernel(axis, count, x_ref, out_ref, sent, landed, own_sem):
+    me = lax.axis_index(axis)
+    barrier = pltpu.get_barrier_semaphore()
+    others = [lax.rem(me + hop, count) for hop in range(1, count)]
+    for other in others:
+        pl.semaphore_signal(barrier, inc=1, device_id={axis: other}, device_id_type=MESH)
+    pl.semaphore_wait(barrier, count - 1)
+
+    def move(hop, block):
+        return pltpu.make_async_remote_copy(
+            src_ref=x_ref,
+            dst_ref=out_ref.at[block],
+            send_sem=sent.at[hop],
+            recv_sem=landed.at[block],
+            device_id={axis: others[hop]},
+            device_id_type=MESH,
+        )
+
+    own = pltpu.make_async_copy(x_ref, out_ref.at[me], own_sem)
+    for hop in range(count - 1):
+        move(hop, me).start()
+    own.start()
+    for hop in range(count - 1):
+        move(hop, others[hop]).wait_recv()
+    for hop in range(count - 1):
+        move(hop, me).wait_send()
+    own.wait()
+
+
+def gather(x, axis, kernel, number):
+    count = lax.axis_size(axis)
+    dma = pltpu.SemaphoreType.DMA
+    sends = [dma((count,))] * (2 if kernel is line_kernel else 1)
+    return pl.pallas_call(
+        functools.partial(kernel, axis, count),
+        in_specs=[pl.BlockSpec(memory_space=pl.ANY)],
+        out_specs=pl.BlockSpec(memory_space=pl.ANY),
+        out_shape=jax.ShapeDtypeStruct((count,) + x.shape, x.dtype),
+        scratch_shapes=sends + [dma((count,)), dma(())],
+        compiler_params=pltpu.CompilerParams(
+            collective_id=number, has_side_effects=True, vmem_limit_bytes=LIMIT
+        ),
+        name="gather_" + axis,
+    )(x)
 
 
 def project_kernel(x_ref, gain_ref, wv_ref, wg_ref, *rest):
@@ -378,16 +482,16 @@
 def body(
     hidden, norm_gain, value_weight, gate_weight, value_taps, gate_taps, rates, residues, out_weight
 ):
-    parts = 2
+    parts = 1
     rows = hidden.shape[0] // parts
     wholes = [
-        lax.all_gather(hidden[part * rows : (part + 1) * rows], "tp", axis=0) for part in range(parts)
+        gather(hidden[part * rows : (part + 1) * rows], "tp", line_kernel, part) for part in range(parts)
     ]
     proj = ()
     for part, whole in enumerate(wholes):
         proj = project(whole, part, parts, norm_gain, value_weight, gate_weight, proj)
     sent, fore, back = local_states(*proj, value_taps, rates)
-    everyone = lax.all_gather(sent, "seq", axis=0)
+    everyone = gather(sent, "seq", direct_kernel, parts)
     place = lax.axis_index("seq").astype(jnp.int32).reshape(1)
     z = gated(place, *proj, value_taps, gate_taps, rates, residues, fore, back, everyone)
     term = output(z, out_weight, lax.axis_size("tp"))

time: 184 us -> 162 us (0.88)
  waiting for transfers between devices: 118 us -> 44.5 us
  Pallas kernels: 50.7 us -> 104 us
  local copies, waits for them, and re-layouts: 1.84 us -> 0 us
    all_gather x3 -> x0, waiting for transfers between devices: 73 us -> none  [the longest x2 48.8 us: body(): lax.all_gather(hidden[part * rows:(part + 1) * rows], 'tp', axis=0)]
    pallas_call x0 -> x2, Pallas kernels: none -> 59.3 us  [gather(): pl.pallas_call(functools.partial(kernel, axis, count), in_specs=[pl.Block...]
    pallas_call x2 -> x1, Pallas kernels: 21.2 us -> 14.8 us  [project(): pl.pallas_call(project_kernel, grid=(chans // size,), in_specs=[pl.BlockS...]
    slice x1 -> x0, local copies, waits for them, and re-layouts: 1.84 us -> none  [body(): hidden[part * rows:(part + 1) * rows]]
  transfers between devices with their start and end apart: 4 -> 1, of which waited for: 4 -> 1; matrix products, arithmetic and copies ran while one was open for 0% -> 0% of each run, Pallas kernels for 6% -> 0%
where the time goes in v2:
time: 162 us
  Pallas kernels  104 us (64%)
  waiting for transfers between devices  44.5 us (27%)
  between operations  13.4 us (8%)
    pallas_call x2, Pallas kernels, gather(): pl.pallas_call(functools.partial(kernel, axis, count), in_specs=[pl.Block...  59.3 us
    reduce_scatter x1, waiting for transfers between devices, body(): return lax.psum_scatter(term, 'tp', scatter_dimension=0, tiled=False)  44.5 us
    pallas_call x1, Pallas kernels, project(): pl.pallas_call(project_kernel, grid=(chans // size,), in_specs=[pl.BlockS...  14.8 us
    pallas_call x1, Pallas kernels, gated(): pl.pallas_call(gated_kernel, grid=(tiles,), in_specs=[pl.BlockSpec(memory...  11.5 us
    pallas_call x1, Pallas kernels, output(): pl.pallas_call(output_kernel, grid=(tiles // 2,), in_specs=[pl.BlockSpec(...  9.69 us
    pallas_call x1, Pallas kernels, local_states(): pl.pallas_call(states_kernel, grid=(tiles,), in_specs=[pl.BlockSpec((2, r...  8.43 us
  transfers between devices with their start and end apart: 1, of which 1 were waited for; matrix products, arithmetic and copies ran while one was open for 0% of the time, Pallas kernels for 0%

profile of v2, /device:TPU:0, one launch (start us, length us, event | category | flops | bytes accessed | tf_op | source)
XLA Modules:
  0.0 161.6 jit_solution(4453224639539464064)
XLA Ops:
  6.5 0.0 reduce-scatter.2.cloned.1.call-start
  6.5 41.8 %gather_tp.1.x_ref = bf16[4,256,1024]{2,1,0:T(8,128)(2,1)} custom-call(bf16[256,1024]{1,0:T(8,128)(2,1)} %x_ref.1), custom_call_target="tpu_custom_call" | custom-call | tf_op jit(solution)/shard_map/gather_tp/pallas_call | solution.py:126
  48.3 14.8 %project.1 = (bf16[2,256,1024]{2,1,0:T(8,128)(2,1)}, bf16[2,256,1024]{2,1,0:T(8,128)(2,1)}) custom-call(bf16[4,256,1024]{2,1,0:T(8,128)(2,1)} %gather_tp.1.x_ref, f32[1,4096]{1,0:T(1,128)} %bitcast.3, bf16[4096,1024]{1,0:T(8,128)(2,1)} %wv_ref.1, bf16[4096,1024]{1,0:T(8,128)(2,1)} %wg_ref.1), custom_call_target="tpu_custom_call" | custom-call | flops 8589934592 | bytes 16777216 | tf_op jit(solution)/shard_map/project/pallas_call | solution.py:171
  63.2 8.4 %local_states.1 = (bf16[80,1024]{1,0:T(8,128)(2,1)}, f32[2,16,16,1024]{3,2,1,0:T(8,128)}, f32[2,16,16,1024]{3,2,1,0:T(8,128)}) custom-call(bf16[2,256,1024]{2,1,0:T(8,128)(2,1)} %get-tuple-element.10.v_ref, bf16[2,256,1024]{2,1,0:T(8,128)(2,1)} %get-tuple-element.11.g_ref, f32[3,1024]{1,0:T(4,128)} %vtaps_ref.1, f32[16,1024]{1,0:T(8,128)} %rates_ref.3), custom_call_target="tpu_custom_call" | custom-call | tf_op jit(solution)/shard_map/local_states/pallas_call | solution.py:275
  71.6 17.5 %gather_seq.1.all_ref = bf16[8,80,1024]{2,1,0:T(8,128)(2,1)} custom-call(bf16[80,1024]{1,0:T(8,128)(2,1)} %get-tuple-element.14.x_ref), custom_call_target="tpu_custom_call" | custom-call | tf_op jit(solution)/shard_map/gather_seq/pallas_call | solution.py:126
  89.1 11.5 %gated.1.z_ref = bf16[2,256,1024]{2,1,0:T(8,128)(2,1)} custom-call(s32[1]{0:T(128)} %bitcast.place_ref, bf16[2,256,1024]{2,1,0:T(8,128)(2,1)} %get-tuple-element.10.v_ref, bf16[2,256,1024]{2,1,0:T(8,128)(2,1)} %get-tuple-element.11.g_ref, f32[3,1024]{1,0:T(4,128)} %vtaps_ref.1, f32[3,1024]{1,0:T(4,128)} %gtaps_ref.1, f32[16,1024]{1,0:T(8,128)} %rates_ref.3, ...), custom_call_target="tpu_custom_call" | custom-call | tf_op jit(solution)/shard_map/gated/pallas_call | solution.py:407
  100.6 9.7 %output.1 = bf16[4,256,1024]{2,1,0:T(8,128)(2,1)} custom-call(bf16[2,256,1024]{2,1,0:T(8,128)(2,1)} %gated.1.z_ref, bf16[1024,4096]{1,0:T(8,128)(2,1)} %high_ref.1, bf16[1024,4096]{1,0:T(8,128)(2,1)} %high_ref.1), custom_call_target="tpu_custom_call" | custom-call | tf_op jit(solution)/shard_map/output/pallas_call | solution.py:467
  110.3 0.0 reduce-scatter.2.cloned.1.call-update
  110.3 44.5 %reduce-scatter.2.cloned.1.call-done = bf16[1,256,1024]{2,1,0:T(8,128)(2,1)} async-done(((bf16[4,256,1024]{2,1,0:T(8,128)(2,1)}), bf16[1,256,1024]{2,1,0:T(8,128)(2,1)}) %reduce-scatter.2.cloned.1.call-update) | async-done | bytes 524304 | tf_op jit(solution)/shard_map/reduce_scatter | solution.py:498
Async XLA Ops:
  6.5 148.2 %reduce-scatter.2.cloned.1.call-start = ((), (), s32[]{:S(2)}) async-start(), calls=%async_computation.1 | async-start | bytes 2621440 | tf_op jit(solution)/shard_map/reduce_scatter | solution.py:498
Sparse Core Ops, SparseCore 0:
  110.4 44.2 reduce-scatter.1

commit v3 on v2

--- a/solution.py
+++ b/solution.py
@@ -134,6 +134,89 @@
         ),
         name="gather_" + axis,
     )(x)
+
+
+def scatter_kernel(axis, count, term_ref, out_ref, from_left, from_right, to_right, to_left, in_left, in_right):
+    me = lax.axis_index(axis)
+    left, right = jnp.maximum(me - 1, 0), jnp.minimum(me + 1, count - 1)
+    barrier = pltpu.get_barrier_semaphore()
+    for hop in range(1, count):
+        other = lax.rem(me + hop, count)
+        pl.semaphore_signal(barrier, inc=1, device_id={axis: other}, device_id_type=MESH)
+    pl.semaphore_wait(barrier, count - 1)
+
+    def move(block, rightward):
+        slots, sends, lands, target = (
+            (from_left, to_right, in_left, right) if rightward else (from_right, to_left, in_right, left)
+        )
+        return pltpu.make_async_remote_copy(
+            src_ref=slots.at[block],
+            dst_ref=slots.at[block],
+            send_sem=sends.at[block],
+            recv_sem=lands.at[block],
+            device_id={axis: target},
+            device_id_type=MESH,
+        )
+
+    def ways(k):
+        return ((count - 1 - k, True), (k, False))
+
+    for k in range(count):
+        for block, rightward in ways(k):
+            slots = from_left if rightward else from_right
+            begins = me == 0 if rightward else me == count - 1
+            passes = me < block if rightward else me > block
+            takes = me <= block if rightward else me >= block
+
+            @pl.when(jnp.logical_and(takes, jnp.logical_not(begins)))
+            def _():
+                move(block, rightward).wait_recv()
+
+            @pl.when(jnp.logical_and(passes, begins))
+            def _():
+                slots[block] = term_ref[block]
+
+            @pl.when(jnp.logical_and(passes, jnp.logical_not(begins)))
+            def _():
+                slots[block] = (slots[block].astype(f32) + term_ref[block].astype(f32)).astype(bf16)
+
+            @pl.when(passes)
+            def _():
+                move(block, rightward).start()
+
+    for block in range(count):
+
+        @pl.when(me == block)
+        def _():
+            total = term_ref[block].astype(f32)
+            if block > 0:
+                total = total + from_left[block].astype(f32)
+            if block < count - 1:
+                total = total + from_right[block].astype(f32)
+            out_ref[...] = total.astype(bf16)
+
+    for k in range(count):
+        for block, rightward in ways(k):
+
+            @pl.when(me < block if rightward else me > block)
+            def _():
+                move(block, rightward).wait_send()
+
+
+def scatter_sum(term, axis, number):
+    count, rows, each = term.shape
+    sems = pltpu.SemaphoreType.DMA((count,))
+    return pl.pallas_call(
+        functools.partial(scatter_kernel, axis, count),
+        in_specs=[pl.BlockSpec(memory_space=pltpu.VMEM)],
+        out_specs=pl.BlockSpec(memory_space=pltpu.VMEM),
+        out_shape=jax.ShapeDtypeStruct((rows, each), term.dtype),
+        scratch_shapes=[pltpu.VMEM(term.shape, term.dtype)] * 2 + [sems] * 4,
+        compiler_params=pltpu.CompilerParams(
+            collective_id=number, has_side_effects=True, vmem_limit_bytes=LIMIT
+        ),
+        name="scatter_sum",
+    )(term)
 
 
 def project_kernel(x_ref, gain_ref, wv_ref, wg_ref, *rest):
@@ -495,7 +578,7 @@
     place = lax.axis_index("seq").astype(jnp.int32).reshape(1)
     z = gated(place, *proj, value_taps, gate_taps, rates, residues, fore, back, everyone)
     term = output(z, out_weight, lax.axis_size("tp"))
-    return lax.psum_scatter(term, "tp", scatter_dimension=0, tiled=False)
+    return scatter_sum(term, "tp", parts + 1)
 
 
 def solution(mesh):

time: 162 us -> 215 us (1.33)
  the two profiles are of different devices: /device:TPU:0 before, /device:TPU:14 now
where the time goes in v3:
time: 215 us; the launch traced here: 214 us
  Pallas kernels  212 us (99%)
    pallas_call x1, Pallas kernels, scatter_sum(): pl.pallas_call(functools.partial(scatter_kernel, axis, count), in_specs=[...  114 us
    pallas_call x2, Pallas kernels, gather(): pl.pallas_call(functools.partial(kernel, axis, count), in_specs=[pl.Block...  53.9 us
    pallas_call x1, Pallas kernels, project(): pl.pallas_call(project_kernel, grid=(chans // size,), in_specs=[pl.BlockS...  14.8 us
    pallas_call x1, Pallas kernels, gated(): pl.pallas_call(gated_kernel, grid=(tiles,), in_specs=[pl.BlockSpec(memory...  11.5 us
    pallas_call x1, Pallas kernels, output(): pl.pallas_call(output_kernel, grid=(tiles // 2,), in_specs=[pl.BlockSpec(...  9.7 us
    pallas_call x1, Pallas kernels, local_states(): pl.pallas_call(states_kernel, grid=(tiles,), in_specs=[pl.BlockSpec((2, r...  8.42 us

profile of v3, /device:TPU:14, one launch (start us, length us, event | category | flops | bytes accessed | tf_op | source)
XLA Modules:
  0.0 214.0 jit_solution(15039984752116618810)
XLA Ops:
  0.0 38.3 %gather_tp.1.x_ref = bf16[4,256,1024]{2,1,0:T(8,128)(2,1)} custom-call(bf16[256,1024]{1,0:T(8,128)(2,1)} %x_ref.1), custom_call_target="tpu_custom_call" | custom-call | tf_op jit(solution)/shard_map/gather_tp/pallas_call | solution.py:126
  38.3 14.8 %project.1 = (bf16[2,256,1024]{2,1,0:T(8,128)(2,1)}, bf16[2,256,1024]{2,1,0:T(8,128)(2,1)}) custom-call(bf16[4,256,1024]{2,1,0:T(8,128)(2,1)} %gather_tp.1.x_ref, f32[1,4096]{1,0:T(1,128)} %bitcast.2, bf16[4096,1024]{1,0:T(8,128)(2,1)} %wv_ref.1, bf16[4096,1024]{1,0:T(8,128)(2,1)} %wg_ref.1), custom_call_target="tpu_custom_call" | custom-call | flops 8589934592 | bytes 16777216 | tf_op jit(solution)/shard_map/project/pallas_call | solution.py:254
  53.2 8.4 %local_states.1 = (bf16[80,1024]{1,0:T(8,128)(2,1)}, f32[2,16,16,1024]{3,2,1,0:T(8,128)}, f32[2,16,16,1024]{3,2,1,0:T(8,128)}) custom-call(bf16[2,256,1024]{2,1,0:T(8,128)(2,1)} %get-tuple-element.10.v_ref, bf16[2,256,1024]{2,1,0:T(8,128)(2,1)} %get-tuple-element.11.g_ref, f32[3,1024]{1,0:T(4,128)} %vtaps_ref.1, f32[16,1024]{1,0:T(8,128)} %rates_ref.3), custom_call_target="tpu_custom_call" | custom-call | tf_op jit(solution)/shard_map/local_states/pallas_call | solution.py:358
  61.6 15.6 %gather_seq.1.all_ref = bf16[8,80,1024]{2,1,0:T(8,128)(2,1)} custom-call(bf16[80,1024]{1,0:T(8,128)(2,1)} %get-tuple-element.14.x_ref), custom_call_target="tpu_custom_call" | custom-call | tf_op jit(solution)/shard_map/gather_seq/pallas_call | solution.py:126
  77.2 11.5 %gated.1.z_ref = bf16[2,256,1024]{2,1,0:T(8,128)(2,1)} custom-call(s32[1]{0:T(128)} %bitcast.place_ref, bf16[2,256,1024]{2,1,0:T(8,128)(2,1)} %get-tuple-element.10.v_ref, bf16[2,256,1024]{2,1,0:T(8,128)(2,1)} %get-tuple-element.11.g_ref, f32[3,1024]{1,0:T(4,128)} %vtaps_ref.1, f32[3,1024]{1,0:T(4,128)} %gtaps_ref.1, f32[16,1024]{1,0:T(8,128)} %rates_ref.3, ...), custom_call_target="tpu_custom_call" | custom-call | tf_op jit(solution)/shard_map/gated/pallas_call | solution.py:490
  88.7 9.7 %output.1.term_ref = bf16[4,256,1024]{2,1,0:T(8,128)(2,1)} custom-call(bf16[2,256,1024]{2,1,0:T(8,128)(2,1)} %gated.1.z_ref, bf16[1024,4096]{1,0:T(8,128)(2,1)} %high_ref.1, bf16[1024,4096]{1,0:T(8,128)(2,1)} %high_ref.1), custom_call_target="tpu_custom_call" | custom-call | tf_op jit(solution)/shard_map/output/pallas_call | solution.py:550
  98.4 113.7 %scatter_sum.1 = bf16[256,1024]{1,0:T(8,128)(2,1)} custom-call(bf16[4,256,1024]{2,1,0:T(8,128)(2,1)} %output.1.term_ref), custom_call_target="tpu_custom_call" | custom-call | tf_op jit(solution)/shard_map/scatter_sum/pallas_call | solution.py:209
  212.1 1.9 copy.11
